TPU v7x, 32 devices: a whole 2x2x4 slice. The times are simulated.
32 devices in a mesh: patch: 8 (over z, core), expert: 4 (over y, x).
Axes of the slice: x: 2, y: 2, z: 4, core: 2. Of those that a mesh axis runs over, the one named last changes fastest.
Arguments:
- latent: bfloat16 [4, 1024, 1152], P('expert', 'patch'), may hold values from -6 to 6
- stale_kv: bfloat16 [4, 1024, 1152], P('expert', 'patch'), may hold values from -300 to 300
- modulation: float32 [1, 6, 1152], replicated, may hold values from -3 to 3
- routes: int32 [1, 4, 1024, 2], P(None, 'expert', 'patch'), may hold values from 0 to 3, all different within a row; in each aligned block of 128 rows (0 to 127, 128 to 255, ..., all dimensions but the last counted through in order) at most 80 rows name the same one
- w_qkv: bfloat16 [1152, 1728], replicated, may hold values from -0.1875 to 0.1875
- w_attn_out: bfloat16 [576, 1152], replicated, may hold values from -0.25 to 0.25
- router: bfloat16 [1152, 4], replicated, may hold values from -0.1875 to 0.1875
- w_in: bfloat16 [4, 1152, 2304], P('expert', 'patch'), may hold values from -0.1875 to 0.1875
- w_out: bfloat16 [4, 2304, 1152], P('expert', 'patch'), may hold values from -0.125 to 0.125
Outputs:
- latent_out: bfloat16 [4, 1024, 1152], P('expert', 'patch')
- fresh_kv: bfloat16 [4, 1024, 1152], P('expert', 'patch')
Inputs may be any that keep to these rules, and one draw needn't show every extreme that they name: A patch's two routes name different experts. In each step, clip and aligned block of 128 patches (the patches of one device) no expert is named by more than 80 routes, and in every draw some block names some expert exactly 80 times.
All inputs are finite; a program needn't handle non-finite values.
Results may differ from a plain program's by a relative error of at most 0.009.
Values may be sent and summed in bfloat16 or wider, within the bound.
A program may use at most 128 MiB of HBM per device.

v0:
```python
import jax
import jax.numpy as jnp
from jax import lax
from jax.sharding import PartitionSpec as P

HEADS = 8


EPSILON = 1e-06


def normalize(values, shift, scale):
    widened = values.astype(jnp.float32)
    center = jnp.mean(widened, axis=-1, keepdims=True)
    spread = jnp.mean(jnp.square(widened - center), axis=-1, keepdims=True)
    return ((widened - center) * lax.rsqrt(spread + EPSILON) * (1.0 + scale) + shift).astype(
        jnp.bfloat16
    )


def attend_keys(query, current, previous, own_start, head_count):
    token_count, attn_width = query.shape
    head_size = attn_width // head_count
    factor = head_size ** (-0.5)
    query_heads = query.reshape(token_count, head_count, head_size)

    def scores_of(kv_rows):
        keys = kv_rows[:, :attn_width].reshape(kv_rows.shape[0], head_count, head_size)
        return (
            jnp.einsum("qhd,khd->hqk", query_heads, keys, preferred_element_type=jnp.float32)
            * factor
        )

    def values_of(kv_rows):
        return kv_rows[:, attn_width:].reshape(kv_rows.shape[0], head_count, head_size)

    own_scores = scores_of(current)
    highest = jnp.max(own_scores, axis=-1)
    weights = jnp.exp(own_scores - highest[..., None])
    totals = jnp.sum(weights, axis=-1)
    summed = jnp.einsum(
        "hqk,khd->hqd",
        weights.astype(jnp.bfloat16),
        values_of(current),
        preferred_element_type=jnp.float32,
    )
    best = highest
    mass = totals
    accum = summed
    rows = lax.all_gather(previous[None], "patch", axis=1, tiled=True)[0]
    positions = jnp.arange(rows.shape[0], dtype=jnp.int32)
    foreign = (positions < own_start) | (positions >= own_start + token_count)
    scores = jnp.where(foreign[None, None, :], scores_of(rows), -1e30)
    renewed = jnp.maximum(best, jnp.max(scores, axis=-1))
    decay = jnp.exp(best - renewed)
    fresh = jnp.exp(scores - renewed[..., None])
    mass = mass * decay + jnp.sum(fresh, axis=-1)
    added = jnp.einsum(
        "hqk,khd->hqd",
        fresh.astype(jnp.bfloat16),
        values_of(rows),
        preferred_element_type=jnp.float32,
    )
    best, mass, accum = (renewed, mass, accum * decay[..., None] + added)
    result = accum / mass[..., None]
    return jnp.transpose(result, (1, 0, 2)).reshape(token_count, attn_width).astype(jnp.bfloat16)


def expert_block(normed, chosen, router, weight_in, weight_out, capacity):
    token_count, width = normed.shape
    expert_count = router.shape[1]
    logits = jnp.dot(normed, router, preferred_element_type=jnp.float32)
    onehot = chosen[..., None] == jnp.arange(expert_count, dtype=jnp.int32)
    gates = jax.nn.sigmoid(jnp.sum(jnp.where(onehot, logits[:, None, :], 0.0), axis=-1))
    flat = onehot.reshape(2 * token_count, expert_count).astype(jnp.int32)
    slots = jnp.sum((jnp.cumsum(flat, axis=0) - flat) * flat, axis=-1)
    targets = chosen.reshape(-1) * capacity + slots
    columns = jnp.arange(expert_count * capacity, dtype=jnp.int32)
    placement = jnp.sum(
        (targets.reshape(token_count, 2)[:, :, None] == columns[None, None, :]).astype(
            jnp.bfloat16
        ),
        axis=1,
    )
    outgoing = jnp.einsum(
        "ts,td->sd", placement, normed, preferred_element_type=jnp.float32
    ).astype(jnp.bfloat16)
    outgoing = outgoing.reshape(expert_count, capacity, width)
    arrived = lax.all_to_all(outgoing, "expert", split_axis=0, concat_axis=0, tiled=True)
    flat_rows = arrived.reshape(expert_count * capacity, width)
    hidden = jax.nn.gelu(
        jnp.dot(flat_rows, weight_in, preferred_element_type=jnp.float32), approximate=True
    ).astype(jnp.bfloat16)
    produced = jnp.dot(hidden, weight_out, preferred_element_type=jnp.float32).astype(jnp.bfloat16)
    returned = lax.all_to_all(
        produced.reshape(expert_count, capacity, width),
        "expert",
        split_axis=0,
        concat_axis=0,
        tiled=True,
    )
    picked = (
        returned.reshape(expert_count * capacity, width)[targets]
        .astype(jnp.float32)
        .reshape(token_count, 2, width)
    )
    return jnp.sum(picked * gates[..., None], axis=1)


def on_device(latent, stale_kv, modulation, routes, w_qkv, w_attn_out, router, w_in, w_out):
    token_count = latent.shape[1]
    attn_width = w_attn_out.shape[0]
    expert_groups = lax.axis_size("expert")
    capacity = min(token_count, 5 * token_count // (2 * expert_groups))
    full_in, full_out = (
        lax.all_gather(w_in, "patch", axis=1, tiled=True),
        lax.all_gather(w_out, "patch", axis=1, tiled=True),
    )
    full_in = full_in[0]
    full_out = full_out[0]
    own_start = lax.axis_index("patch") * token_count
    state = latent[0]
    previous = stale_kv[0]
    shifts = modulation[0]
    normed = normalize(state, shifts[0], shifts[1])
    merged = jnp.dot(normed, w_qkv, preferred_element_type=jnp.float32).astype(jnp.bfloat16)
    query = merged[:, :attn_width]
    current = merged[:, attn_width:]
    attended = attend_keys(query, current, previous, own_start, HEADS)
    projected = jnp.dot(attended, w_attn_out, preferred_element_type=jnp.float32)
    middle = (state.astype(jnp.float32) + shifts[2] * projected).astype(jnp.bfloat16)
    normed_two = normalize(middle, shifts[3], shifts[4])
    mixture = expert_block(normed_two, routes[0, 0], router, full_in, full_out, capacity)
    state = (middle.astype(jnp.float32) + shifts[5] * mixture).astype(jnp.bfloat16)
    return (state[None], current[None])


def solution(mesh):
    in_specs = (
        P("expert", "patch", None),
        P("expert", "patch", None),
        P(),
        P(None, "expert", "patch", None),
        P(),
        P(),
        P(),
        P("expert", "patch", None),
        P("expert", "patch", None),
    )
    out_specs = (P("expert", "patch", None), P("expert", "patch", None))
    return jax.shard_map(
        on_device, mesh=mesh, in_specs=in_specs, out_specs=out_specs, check_vma=False
    )
```

profile of v0, /device:TPU:1, one launch (start us, length us, event | category | flops | bytes accessed | tf_op | source)
XLA Modules:
  0.0 190.7 jit_solution(4968174803787740564)
XLA Ops:
  10.5 1.2 reduce-window.6
  13.5 1.4 slice_reduce_fusion.1
  15.6 1.1 convert_reduce_fusion
  16.6 1.2 fusion.38
  17.9 3.6 %convolution_convert_fusion.1 = bf16[128,1728]{0,1:T(8,128)(2,1)S(1)} fusion(bf16[1152,1728]{0,1:T(8,128)(2,1)} %param.13, bf16[1,128,1152]{2,1,0:T(8,128)(2,1)S(1)} %copy-done.2, f32[1152]{0:T(1024)S(1)} %get-tuple-element.9, f32[1152]{0:T(1024)S(1)} %get-tuple-element.10, f32[128]{0:T(128)S(1)} %add_rsqrt_fusion.1, f32[128]{0:T(128)S(1)} %broadcast_multiply_fusion.2), kind=kOutput, calls=%fused_computation.23 | convolution fusion | flops 510713856 | bytes 4728832 | tf_op jit(solution)/shard_map/dot_general | solution.py:126
  23.8 20.0 %all-gather.4.cloned.1.call-done = bf16[1,1024,1152]{2,1,0:T(8,128)(2,1)} async-done(((bf16[1,128,1152]{2,1,0:T(8,128)(2,1)}), bf16[1,1024,1152]{2,1,0:T(8,128)(2,1)}) %all-gather.4.cloned.1.call-update) | async-done | bytes 2359312 | tf_op jit(solution)/shard_map/all_gather | solution.py:50
  43.9 3.5 %fusion.62 = (bf16[1024,576]{1,0:T(8,128)(2,1)}, bf16[1024,576]{1,0:T(8,128)(2,1)S(1)}) fusion(bf16[1024,1152]{1,0:T(8,128)(2,1)} %bitcast.116), kind=kLoop, calls=%fused_computation.94 | loop fusion | bytes 4718592 | tf_op jit(solution)/shard_map/slice | solution.py:28
  47.3 2.4 %copy.32 = bf16[1024,576]{0,1:T(8,128)(2,1)} copy(bf16[1024,576]{1,0:T(8,128)(2,1)} %get-tuple-element.16) | data formatting | bytes 2359296 | tf_op jit(solution)/shard_map/slice | solution.py:28
  49.8 4.2 %fusion.4 = (f32[8,128]{1,0:T(8,128)S(1)}, f32[8,128,1024]{2,1,0:T(8,128)}) fusion(pred[1024]{0:T(1024)(128)(4,1)} %fusion.58, bf16[128,8,72]{0,2,1:T(8,128)(2,1)} %bitcast.119, bf16[1024,8,72]{0,2,1:T(8,128)(2,1)} %bitcast.115), kind=kOutput, calls=%fused_computation.8 | convolution fusion | flops 154139648 | bytes 5526528 | tf_op jit(solution)/shard_map/qhd,khd->hqk/dot_general | solution.py:30
  54.6 1.5 copy.33
  56.0 3.3 %fusion.5 = f32[8,128]{1,0:T(8,128)S(1)} fusion(f32[8,128,1024]{2,1,0:T(8,128)} %get-tuple-element.24, f32[8,128]{1,0:T(8,128)} %max.18, pred[1024]{0:T(1024)(128)(4,1)} %fusion.58), kind=kLoop, calls=%fused_computation.9 | loop fusion | flops 4193280 | bytes 4203520 | tf_op jit(solution)/shard_map/reduce_sum | solution.py:57
  59.5 2.4 %fusion.28 = f32[128,8,72]{0,2,1:T(8,128)S(1)} fusion(bf16[1024,8,72]{0,2,1:T(8,128)(2,1)} %bitcast.120, f32[8,128,1024]{2,1,0:T(8,128)S(1)} %copy-done.1, f32[8,128]{1,0:T(8,128)S(1)} %copy-done.8, pred[1024]{0:T(1024)(128)(4,1)S(1)} %copy-done.13), kind=kOutput, calls=%fused_computation.30 | convolution fusion | flops 155189248 | bytes 5673984 | tf_op jit(solution)/shard_map/hqk,khd->hqd/dot_general | solution.py:58
  63.2 1.2 convolution_convert_fusion
  64.5 3.5 %all-to-all-start = ((bf16[4,80,1152]{2,1,0:T(8,128)(2,1)}), bf16[4,80,1152]{2,1,0:T(8,128)(2,1)S(1)}, u32[]{:S(2)}, u32[]{:S(2)}) async-start(bf16[4,80,1152]{2,1,0:T(8,128)(2,1)} %bitcast.17), calls=%async_computation | async-start | bytes 1474560 | tf_op jit(solution)/shard_map/all_to_all | solution.py:89
  69.2 8.8 %all-to-all-done = bf16[4,80,1152]{2,1,0:T(8,128)(2,1)S(1)} async-done(((bf16[4,80,1152]{2,1,0:T(8,128)(2,1)}), bf16[4,80,1152]{2,1,0:T(8,128)(2,1)S(1)}, u32[]{:S(2)}, u32[]{:S(2)}) %all-to-all-start) | async-done | bytes 737312 | tf_op jit(solution)/shard_map/all_to_all | solution.py:89
  78.0 23.3 %all-gather.6.cloned.1.call-done = bf16[1,1152,2304]{2,1,0:T(8,128)(2,1)} async-done(((bf16[1,144,2304]{2,1,0:T(8,128)(2,1)}), bf16[1,1152,2304]{2,1,0:T(8,128)(2,1)}) %all-gather.6.cloned.1.call-update) | async-done | bytes 5308432 | tf_op jit(solution)/shard_map/all_gather | solution.py:116
  101.3 6.0 %fusion.16 = bf16[320,2304]{1,0:T(8,128)(2,1)} fusion(bf16[320,1152]{1,0:T(8,128)(2,1)S(1)} %bitcast.121, bf16[1,1152,2304]{2,1,0:T(8,128)(2,1)} %all-gather.6.cloned.1.call-done), kind=kOutput, calls=%fused_computation.18 | convolution fusion | flops 1705328640 | bytes 7520256 | tf_op jit(solution)/shard_map/dot_general | solution.py:92
  107.3 51.0 %all-gather.8.cloned.1.call-done = bf16[1,2304,1152]{2,1,0:T(8,128)(2,1)} async-done(((bf16[1,288,1152]{2,1,0:T(8,128)(2,1)}), bf16[1,2304,1152]{2,1,0:T(8,128)(2,1)}) %all-gather.8.cloned.1.call-update) | async-done | bytes 5308432 | tf_op jit(solution)/shard_map/all_gather | solution.py:117
  158.3 5.9 %fusion.19 = bf16[320,1152]{1,0:T(8,128)(2,1)} fusion(bf16[320,2304]{1,0:T(8,128)(2,1)} %fusion.16, bf16[1,2304,1152]{2,1,0:T(8,128)(2,1)} %all-gather.8.cloned.1.call-done), kind=kOutput, calls=%fused_computation.19 | convolution fusion | flops 1699061760 | bytes 7520256 | tf_op jit(solution)/shard_map/dot_general | solution.py:94
  164.2 3.7 %all-to-all-start.1 = ((bf16[4,80,1152]{2,1,0:T(8,128)(2,1)}), bf16[4,80,1152]{2,1,0:T(8,128)(2,1)S(1)}, u32[]{:S(2)}, u32[]{:S(2)}) async-start(bf16[4,80,1152]{2,1,0:T(8,128)(2,1)} %bitcast.122), calls=%async_computation.1 | async-start | bytes 1474560 | tf_op jit(solution)/shard_map/all_to_all | solution.py:95
  168.3 9.7 %all-to-all-done.1 = bf16[4,80,1152]{2,1,0:T(8,128)(2,1)S(1)} async-done(((bf16[4,80,1152]{2,1,0:T(8,128)(2,1)}), bf16[4,80,1152]{2,1,0:T(8,128)(2,1)S(1)}, u32[]{:S(2)}, u32[]{:S(2)}) %all-to-all-start.1) | async-done | bytes 737312 | tf_op jit(solution)/shard_map/all_to_all | solution.py:95
  178.0 2.1 %gather_fusion = bf16[256,1152]{1,0:T(8,128)(2,1)} fusion(bf16[320,1152]{1,0:T(8,128)(2,1)S(1)} %bitcast.114, s32[1024]{0:T(1024)S(1)} %pad_clamp_fusion), kind=kCustom, calls=%fused_computation | custom fusion | bytes 1180672 | tf_op jit(solution)/shard_map/gather | solution.py:103
  180.1 1.9 reshape.190
  182.0 1.5 multiply_reduce_fusion
  (78 shorter events, 12.4 us)
Async XLA Ops:
  7.2 55.1 %copy-start = (bf16[576,1152]{1,0:T(8,128)(2,1)S(1)}, bf16[576,1152]{1,0:T(8,128)(2,1)}, u32[]{:S(2)}) copy-start(bf16[576,1152]{1,0:T(8,128)(2,1)} %param.14) | copy-start | bytes 3981316
  7.2 10.7 %copy-start.2 = (bf16[1,128,1152]{2,1,0:T(8,128)(2,1)S(1)}, bf16[1,128,1152]{2,1,0:T(8,128)(2,1)}, u32[]{:S(2)}) copy-start(bf16[1,128,1152]{2,1,0:T(8,128)(2,1)} %param.9) | copy-start | bytes 884740
  7.2 36.7 %all-gather.4.cloned.1.call-start = ((), (), s32[]{:S(2)}) async-start(), calls=%async_computation.2 | async-start | bytes 2654208 | tf_op jit(solution)/shard_map/all_gather | solution.py:50
  7.9 93.3 %all-gather.6.cloned.1.call-start = ((), (), s32[]{:S(2)}) async-start(), calls=%async_computation.3 | async-start | bytes 5971968 | tf_op jit(solution)/shard_map/all_gather | solution.py:116
  8.7 149.6 %all-gather.8.cloned.1.call-start = ((), (), s32[]{:S(2)}) async-start(), calls=%async_computation.4 | async-start | bytes 5971968 | tf_op jit(solution)/shard_map/all_gather | solution.py:117
  12.1 0.5 copy-start.10
  22.1 21.7 %copy-start.3 = (bf16[128,576]{0,1:T(8,128)(2,1)}, bf16[128,576]{0,1:T(8,128)(2,1)S(1)}, u32[]{:S(2)}) copy-start(bf16[128,576]{0,1:T(8,128)(2,1)S(1)} %get-tuple-element.20) | copy-start | bytes 442372
  56.0 3.4 %copy-start.9 = (f32[8,128]{1,0:T(8,128)S(1)}, f32[8,128]{1,0:T(8,128)}, u32[]{:S(2)}) copy-start(f32[8,128]{1,0:T(8,128)} %fusion.42) | copy-start | bytes 12292
  56.0 3.5 %copy-start.1 = (f32[8,128,1024]{2,1,0:T(8,128)S(1)}, f32[8,128,1024]{2,1,0:T(8,128)}, u32[]{:S(2)}) copy-start(f32[8,128,1024]{2,1,0:T(8,128)} %get-tuple-element.24) | copy-start | bytes 12582916
  56.0 3.5 %copy-start.8 = (f32[8,128]{1,0:T(8,128)S(1)}, f32[8,128]{1,0:T(8,128)}, u32[]{:S(2)}) copy-start(f32[8,128]{1,0:T(8,128)} %max.18) | copy-start | bytes 12292
  56.0 3.5 %copy-start.13 = (pred[1024]{0:T(1024)(128)(4,1)S(1)}, pred[1024]{0:T(1024)(128)(4,1)}, u32[]{:S(2)}) copy-start(pred[1024]{0:T(1024)(128)(4,1)} %fusion.58) | copy-start | bytes 3076
  59.5 2.4 %copy-start.6 = (bf16[128,576]{0,1:T(8,128)(2,1)S(1)}, bf16[128,576]{0,1:T(8,128)(2,1)}, u32[]{:S(2)}) copy-start(bf16[128,576]{0,1:T(8,128)(2,1)} %get-tuple-element.18) | copy-start | bytes 442372
  59.5 2.7 %copy-start.7 = (f32[1152]{0:T(1024)S(1)}, f32[1152]{0:T(1024)}, u32[]{:S(2)}) copy-start(f32[1152]{0:T(1024)} %get-tuple-element.11) | copy-start | bytes 13828
  62.0 1.3 copy-start.5
  62.2 5.7 %copy-start.14 = (s32[1,1,128,2]{2,3,1,0:T(2,128)S(1)}, s32[1,1,128,2]{2,3,1,0:T(2,128)}, u32[]{:S(2)}) copy-start(s32[1,1,128,2]{2,3,1,0:T(2,128)} %param.12) | copy-start | bytes 3076
  62.3 6.0 %copy-start.4 = (bf16[1,128,1152]{1,2,0:T(8,128)(2,1)S(1)}, bf16[1,128,1152]{1,2,0:T(8,128)(2,1)}, u32[]{:S(2)}) copy-start(bf16[1,128,1152]{1,2,0:T(8,128)(2,1)} %slice_bitcast_fusion) | copy-start | bytes 884740
  62.8 6.4 %copy-start.11 = (s32[256]{0:T(256)S(1)}, s32[256]{0:T(256)}, u32[]{:S(2)}) copy-start(s32[256]{0:T(256)} %copy-done.10) | copy-start | bytes 3076
  64.5 13.5 %all-to-all-start = ((bf16[4,80,1152]{2,1,0:T(8,128)(2,1)}), bf16[4,80,1152]{2,1,0:T(8,128)(2,1)S(1)}, u32[]{:S(2)}, u32[]{:S(2)}) async-start(bf16[4,80,1152]{2,1,0:T(8,128)(2,1)} %bitcast.17), calls=%async_computation | async-start | bytes 1474560 | tf_op jit(solution)/shard_map/all_to_all | solution.py:89
  107.3 60.6 %copy-start.12 = (bf16[1152,4]{0,1:T(4,128)(2,1)S(1)}, bf16[1152,4]{0,1:T(4,128)(2,1)}, u32[]{:S(2)}) copy-start(bf16[1152,4]{0,1:T(4,128)(2,1)} %param.15) | copy-start | bytes 27652
  164.2 13.8 %all-to-all-start.1 = ((bf16[4,80,1152]{2,1,0:T(8,128)(2,1)}), bf16[4,80,1152]{2,1,0:T(8,128)(2,1)S(1)}, u32[]{:S(2)}, u32[]{:S(2)}) async-start(bf16[4,80,1152]{2,1,0:T(8,128)(2,1)} %bitcast.122), calls=%async_computation.1 | async-start | bytes 1474560 | tf_op jit(solution)/shard_map/all_to_all | solution.py:95
Sparse Core Ops, SparseCore 0:
  9.7 34.1 all-gather.3
  45.5 55.6 all-gather.5
  102.9 55.3 all-gather.7
where the time goes:
time: 192 us; the launch traced here: 191 us
  waiting for transfers between devices  115 us (60%)
  matrix products  24.6 us (13%)
  local copies, waits for them, and re-layouts  16.3 us (8%)
  between operations  14 us (7%)
  other arithmetic  13.7 us (7%)
  starting transfers between devices  7.27 us (4%)
    all_gather x1, waiting for transfers between devices, on_device(): lax.all_gather(w_out, 'patch', axis=1, tiled=True)  51 us
    all_gather x1, waiting for transfers between devices, on_device(): lax.all_gather(w_in, 'patch', axis=1, tiled=True)  23.3 us
    all_gather x1, waiting for transfers between devices, attend_keys(): rows = lax.all_gather(previous[None], 'patch', axis=1, tiled=True)[0]  20 us
    all_to_all x1, waiting for transfers between devices, expert_block(): lax.all_to_all(produced.reshape(expert_count, capacity, width), 'expert',...  9.74 us
    all_to_all x1, waiting for transfers between devices, expert_block(): lax.all_to_all(outgoing, 'expert', split_axis=0, concat_axis=0, tiled=True)  8.76 us
    dot_general x1, matrix products, expert_block(): jnp.dot(flat_rows, weight_in, preferred_element_type=jnp.float32)  6 us
    dot_general x1, matrix products, expert_block(): jnp.dot(hidden, weight_out, preferred_element_type=jnp.float32)  5.93 us
    slice x2, local copies, waits for them, and re-layouts, scores_of(): kv_rows[:, :attn_width].reshape(kv_rows.shape[0], head_count, head_size)  5.88 us
  transfers between devices with their start and end apart: 5, of which 5 were waited for; matrix products, arithmetic and copies ran while one was open for 22% of the time, Pallas kernels for 0%

commit v1 on v0

--- a/solution.py
+++ b/solution.py
@@ -1,6 +1,10 @@
+import functools
+
 import jax
 import jax.numpy as jnp
 from jax import lax
+from jax.experimental import pallas as pl
+from jax.experimental.pallas import tpu as pltpu
 from jax.sharding import PartitionSpec as P
 
 HEADS = 8
@@ -135,7 +139,389 @@
     return (state[None], current[None])
 
 
+MESH = pl.DeviceIdType.MESH
+TO_PARTNER, TO_MIDDLE, TO_CORE = 0, 1, 2
+
+
+def block_kernel(
+    capacity,
+    latent_ref, stale_ref, mod_ref, routes_ref, wqkv_hbm, wattn_hbm, router_ref, win_hbm, wout_hbm,
+    out_ref, fresh_ref,
+    kv, wqkv, wattn, win, wout, outgoing, rows, hidden, partial, produced, returned, attended,
+    load_sem, send_sem, recv_sem, go_send, go_recv, back_send, back_recv,
+):
+    patch, expert = lax.axis_index("patch"), lax.axis_index("expert")
+    z, core = patch // 2, patch % 2
+    other = z * 2 + (1 - core)
+    partner = (z + 1 - 2 * (z % 2)) * 2 + core
+    across = (3 - z) * 2 + core
+    far = (3 - partner // 2) * 2 + core
+    middle_plane = (z == 1) | (z == 2)
+    end_plane = (z == 0) | (z == 3)
+    tokens, width = latent_ref.shape
+    attn = wattn_hbm.shape[0]
+    head_size = attn // HEADS
+    experts = router_ref.shape[1]
+    ffw = win_hbm.shape[1]
+
+    buffers = (kv, win, wout)
+    owned = (stale_ref, win_hbm, wout_hbm)
+
+    def slot(which, index):
+        count = owned[which].shape[0]
+        return buffers[which].at[pl.ds(pl.multiple_of(index * count, 16), count)]
+
+    def transfer(which, kind, index, own=False):
+        target = (partner, across, other)[kind]
+        return pltpu.make_async_remote_copy(
+            src_ref=owned[which] if own else slot(which, index),
+            dst_ref=slot(which, index),
+            send_sem=send_sem.at[which, kind, index],
+            recv_sem=recv_sem.at[which, index],
+            device_id=(target, expert),
+            device_id_type=MESH,
+        )
+
+    def arrived(which, index):
+        transfer(which, TO_CORE, index).wait_recv()
+
+    load_qkv = pltpu.make_async_copy(wqkv_hbm, wqkv, load_sem.at[0])
+    load_attn = pltpu.make_async_copy(
+        wattn_hbm, wattn.at[pl.ds(wattn.shape[0] - attn, attn)], load_sem.at[1]
+    )
+    load_qkv.start()
+    load_attn.start()
+    own_in = pltpu.make_async_copy(win_hbm, slot(1, patch), load_sem.at[2])
+    own_out = pltpu.make_async_copy(wout_hbm, slot(2, patch), load_sem.at[3])
+
+    @pl.when(middle_plane)
+    def _():
+        own_in.start()
+        own_out.start()
+
+    barrier = pltpu.get_barrier_semaphore()
+    peers = [(other, expert), (partner, expert), (across, expert)]
+    for step in range(1, experts):
+        peers.append((patch, (expert + step) % experts))
+        peers.append((partner, (expert + step) % experts))
+    for peer in peers:
+        pl.semaphore_signal(barrier, inc=1, device_id=peer, device_id_type=MESH)
+    pl.semaphore_wait(barrier, len(peers))
+
+    transfer(0, TO_PARTNER, patch, True).start()
+    transfer(0, TO_CORE, patch, True).start()
+
+    @pl.when(middle_plane)
+    def _():
+        transfer(0, TO_MIDDLE, patch, True).start()
+
+    @pl.when(end_plane)
+    def _():
+        transfer(1, TO_PARTNER, patch, True).start()
+        transfer(2, TO_PARTNER, patch, True).start()
+
+    def row_of(index):
+        return mod_ref[index : index + 1, :]
+
+    normed = normalize(latent_ref[...], row_of(0), row_of(1))
+    load_qkv.wait()
+    merged = jnp.dot(normed, wqkv[...], preferred_element_type=jnp.float32)
+    query = merged[:, : wattn.shape[0]].astype(jnp.bfloat16)
+    current = merged[:, attn:].astype(jnp.bfloat16)
+    fresh_ref[...] = current
+    kv[pl.ds(pl.multiple_of(patch * tokens, 16), tokens), :] = current
+
+    @pl.when(middle_plane)
+    def _():
+        arrived(0, partner)
+        transfer(0, TO_MIDDLE, partner).start()
+        transfer(0, TO_CORE, partner).start()
+        arrived(0, across)
+        transfer(0, TO_PARTNER, across).start()
+        transfer(0, TO_CORE, across).start()
+        transfer(1, TO_MIDDLE, patch, True).start()
+        transfer(1, TO_CORE, patch, True).start()
+        arrived(0, far)
+        transfer(0, TO_PARTNER, far).start()
+        transfer(0, TO_CORE, far).start()
+        transfer(2, TO_MIDDLE, patch, True).start()
+        transfer(2, TO_CORE, patch, True).start()
+
+    @pl.when(end_plane)
+    def _():
+        for index in (partner, far, across):
+            arrived(0, index)
+            transfer(0, TO_CORE, index).start()
+
+    for plane in range(4):
+        arrived(0, plane * 2 + 1 - core)
+
+    lead = wattn.shape[0] - attn
+    base = attn - lead
+    for head in range(HEADS):
+        low, high = head * head_size, (head + 1) * head_size
+        start, stop = low // 128 * 128, -(-high // 128) * 128
+        column = lax.broadcasted_iota(jnp.int32, (tokens, stop - start), 1) + start
+        chosen = jnp.where(
+            (column >= low) & (column < high), query[:, start:stop].astype(jnp.float32), 0.0
+        ).astype(jnp.bfloat16)
+        scores = lax.dot_general(
+            chosen, kv[:, start:stop], (((1,), (1,)), ((), ())), preferred_element_type=jnp.float32
+        ) * head_size ** (-0.5)
+        weights = jnp.exp(scores - jnp.max(scores, axis=-1, keepdims=True))
+        total = jnp.sum(weights, axis=-1, keepdims=True)
+        low, high = attn + low, attn + high
+        start, stop = low // 128 * 128, -(-high // 128) * 128
+        summed = (
+            jnp.dot(
+                weights.astype(jnp.bfloat16), kv[:, start:stop], preferred_element_type=jnp.float32
+            )
+            / total
+        )
+        column = lax.broadcasted_iota(jnp.int32, (tokens, stop - start), 1) + start
+        mine = jnp.where((column >= low) & (column < high), summed, 0.0)
+        first = start - base
+        old = attended[:, first : first + stop - start]
+        keep = (column < low) & (column >= attn)
+        attended[:, first : first + stop - start] = jnp.where(keep, old, mine)
+
+    @pl.when(middle_plane)
+    def _():
+        arrived(1, partner)
+        transfer(1, TO_MIDDLE, partner).start()
+        transfer(1, TO_CORE, partner).start()
+
+    load_attn.wait()
+    wattn[:lead, :] = jnp.zeros((lead, width), jnp.bfloat16)
+    projected = jnp.dot(
+        attended[...].astype(jnp.bfloat16), wattn[...], preferred_element_type=jnp.float32
+    )
+    middle = (latent_ref[...].astype(jnp.float32) + row_of(2) * projected).astype(jnp.bfloat16)
+    out_ref[...] = middle
+    normed_two = normalize(middle, row_of(3), row_of(4))
+    logits = jnp.dot(normed_two, router_ref[...], preferred_element_type=jnp.float32)
+
+    lane = lax.broadcasted_iota(jnp.int32, (tokens, 128), 1)
+    line = lax.broadcasted_iota(jnp.int32, (tokens, tokens), 0)
+    before = lax.broadcasted_iota(jnp.int32, (tokens, tokens), 1) < line
+    named = ((routes_ref[:, 0:1] == lane) | (routes_ref[:, 1:2] == lane)).astype(jnp.float32)
+    place = jnp.dot(
+        before.astype(jnp.float32).astype(jnp.bfloat16),
+        named.astype(jnp.bfloat16),
+        preferred_element_type=jnp.float32,
+    )
+    place = jnp.where(named > 0.0, place, -1.0)
+    place_t = place.T
+    entry = lax.broadcasted_iota(jnp.int32, (capacity, tokens), 0).astype(jnp.float32)
+    for index in range(experts):
+        pick = (entry == place_t[index : index + 1, :]).astype(jnp.float32).astype(jnp.bfloat16)
+        outgoing[index * capacity : (index + 1) * capacity, :] = jnp.dot(
+            pick, normed_two, preferred_element_type=jnp.float32
+        ).astype(jnp.bfloat16)
+
+    def span(index):
+        return pl.ds(pl.multiple_of(index * capacity, 16), capacity)
+
+    def go(side, index):
+        return pltpu.make_async_remote_copy(
+            src_ref=outgoing.at[span(index)],
+            dst_ref=rows.at[span(side * experts + expert)],
+            send_sem=go_send.at[index],
+            recv_sem=go_recv.at[side, expert],
+            device_id=(partner if side else patch, index),
+            device_id_type=MESH,
+        )
+
+    def back(side, index):
+        return pltpu.make_async_remote_copy(
+            src_ref=produced.at[span(side * experts + index)],
+            dst_ref=returned.at[span(expert)],
+            send_sem=back_send.at[side, index],
+            recv_sem=back_recv.at[expert],
+            device_id=(partner if side else patch, index),
+            device_id_type=MESH,
+        )
+
+    def await_rows(side, source):
+        pltpu.make_async_copy(
+            outgoing.at[span(source)],
+            rows.at[span(side * experts + source)],
+            go_recv.at[side, source],
+        ).wait()
+
+    def await_back(source):
+        pltpu.make_async_copy(
+            outgoing.at[span(source)], returned.at[span(source)], back_recv.at[source]
+        ).wait()
+
+    @pl.when(end_plane)
+    def _():
+        for step in range(experts):
+            go(1, (expert + step) % experts).start()
+
+    @pl.when(middle_plane)
+    def _():
+        for step in range(1, experts):
+            go(0, (expert + step) % experts).start()
+        rows[span(expert), :] = outgoing[span(expert), :]
+        arrived(2, partner)
+        transfer(2, TO_MIDDLE, partner).start()
+        transfer(2, TO_CORE, partner).start()
+        for which in (1,):
+            for index in (across, far):
+                arrived(which, index)
+                transfer(which, TO_CORE, index).start()
+        own_in.wait()
+        own_out.wait()
+        for step in range(1, experts):
+            await_rows(0, (expert + step) % experts)
+        for step in range(experts):
+            await_rows(1, (expert + step) % experts)
+        for plane in range(4):
+            arrived(1, plane * 2 + 1 - core)
+
+        def first_layer(step, carry):
+            columns = pl.ds(pl.multiple_of(step * 256, 256), 256)
+            hidden[:, columns] = jax.nn.gelu(
+                jnp.dot(rows[...], win[:, columns], preferred_element_type=jnp.float32),
+                approximate=True,
+            ).astype(jnp.bfloat16)
+            return carry
+
+        lax.fori_loop(0, ffw // 256, first_layer, 0)
+
+        half = ffw // 2
+        near_at = pl.multiple_of((z // 2) * half, 128)
+        far_at = pl.multiple_of((1 - z // 2) * half, 128)
+        arrived(2, other)
+        arrived(2, partner + 1 - 2 * core)
+        partial[...] = jnp.dot(
+            hidden[:, pl.ds(near_at, half)],
+            wout[pl.ds(near_at, half), :],
+            preferred_element_type=jnp.float32,
+        )
+        for index in (across, far):
+            arrived(2, index)
+            transfer(2, TO_CORE, index).start()
+        arrived(2, across + 1 - 2 * core)
+        arrived(2, far + 1 - 2 * core)
+        count = experts * capacity
+        for side in (1, 0):
+            block = slice(side * count, (side + 1) * count)
+            produced[block, :] = (
+                partial[block, :]
+                + jnp.dot(
+                    hidden[block, pl.ds(far_at, half)],
+                    wout[pl.ds(far_at, half), :],
+                    preferred_element_type=jnp.float32,
+                )
+            ).astype(jnp.bfloat16)
+            for step in range(1 - side, experts):
+                back(side, (expert + step) % experts).start()
+        returned[span(expert), :] = produced[span(expert), :]
+        for step in range(1, experts):
+            await_back((expert + step) % experts)
+
+    @pl.when(end_plane)
+    def _():
+        for step in range(experts):
+            await_back((expert + step) % experts)
+
+    mixture = jnp.zeros((tokens, width), jnp.float32)
+    entry = lax.broadcasted_iota(jnp.int32, (tokens, capacity), 1).astype(jnp.float32)
+    gates = jax.nn.sigmoid(logits)
+    for index in range(experts):
+        pick = (entry == place[:, index : index + 1]).astype(jnp.float32).astype(jnp.bfloat16)
+        picked = jnp.dot(
+            pick,
+            returned[index * capacity : (index + 1) * capacity, :],
+            preferred_element_type=jnp.float32,
+        )
+        mixture = mixture + picked * gates[:, index : index + 1]
+    out_ref[...] = (out_ref[...].astype(jnp.float32) + row_of(5) * mixture).astype(jnp.bfloat16)
+
+    transfer(0, TO_PARTNER, patch, True).wait_send()
+    transfer(0, TO_CORE, patch, True).wait_send()
+    for index in (partner, across, far):
+        transfer(0, TO_CORE, index).wait_send()
+
+    @pl.when(end_plane)
+    def _():
+        transfer(1, TO_PARTNER, patch, True).wait_send()
+        transfer(2, TO_PARTNER, patch, True).wait_send()
+        for step in range(experts):
+            go(1, (expert + step) % experts).wait_send()
+
+    @pl.when(middle_plane)
+    def _():
+        transfer(0, TO_MIDDLE, patch, True).wait_send()
+        transfer(0, TO_MIDDLE, partner).wait_send()
+        transfer(0, TO_PARTNER, across).wait_send()
+        transfer(0, TO_PARTNER, far).wait_send()
+        for which in (1, 2):
+            transfer(which, TO_MIDDLE, patch, True).wait_send()
+            transfer(which, TO_MIDDLE, partner).wait_send()
+            transfer(which, TO_CORE, patch, True).wait_send()
+            for index in (partner, across, far):
+                transfer(which, TO_CORE, index).wait_send()
+        for step in range(1, experts):
+            go(0, (expert + step) % experts).wait_send()
+            back(0, (expert + step) % experts).wait_send()
+        for step in range(experts):
+            back(1, (expert + step) % experts).wait_send()
+
+
+def on_line(latent, stale_kv, modulation, routes, w_qkv, w_attn_out, router, w_in, w_out):
+    tokens, width = latent.shape[1:]
+    attn = w_attn_out.shape[0]
+    experts, patches = lax.axis_size("expert"), lax.axis_size("patch")
+    capacity = min(tokens, 5 * tokens // (2 * experts))
+    ffw = w_in.shape[2]
+    padded = -(-attn // 128) * 128
+    slots = experts * capacity
+    vmem, hbm = pl.BlockSpec(memory_space=pltpu.VMEM), pl.BlockSpec(memory_space=pl.ANY)
+    narrow = jnp.bfloat16
+    state, current = pl.pallas_call(
+        functools.partial(block_kernel, capacity),
+        out_shape=(
+            jax.ShapeDtypeStruct((tokens, width), narrow),
+            jax.ShapeDtypeStruct((tokens, 2 * attn), narrow),
+        ),
+        in_specs=[vmem, hbm, vmem, vmem, hbm, hbm, vmem, hbm, hbm],
+        out_specs=(vmem, vmem),
+        scratch_shapes=[
+            pltpu.VMEM((patches * tokens, 2 * attn), narrow),
+            pltpu.VMEM(w_qkv.shape, narrow),
+            pltpu.VMEM((padded, width), narrow),
+            pltpu.VMEM((width, ffw), narrow),
+            pltpu.VMEM((ffw, width), narrow),
+            pltpu.VMEM((slots, width), narrow),
+            pltpu.VMEM((2 * slots, width), narrow),
+            pltpu.VMEM((2 * slots, ffw), narrow),
+            pltpu.VMEM((2 * slots, width), jnp.float32),
+            pltpu.VMEM((2 * slots, width), narrow),
+            pltpu.VMEM((slots, width), narrow),
+            pltpu.VMEM((tokens, padded), jnp.float32),
+            pltpu.SemaphoreType.DMA((4,)),
+            pltpu.SemaphoreType.DMA((3, 3, patches)),
+            pltpu.SemaphoreType.DMA((3, patches)),
+            pltpu.SemaphoreType.DMA((experts,)),
+            pltpu.SemaphoreType.DMA((2, experts)),
+            pltpu.SemaphoreType.DMA((2, experts)),
+            pltpu.SemaphoreType.DMA((experts,)),
+        ],
+        compiler_params=pltpu.CompilerParams(
+            collective_id=0, has_side_effects=True, vmem_limit_bytes=56 * 1024 * 1024
+        ),
+    )(
+        latent[0], stale_kv[0], modulation[0], routes[0, 0], w_qkv, w_attn_out, router,
+        w_in[0], w_out[0],
+    )
+    return (state[None], current[None])
+
+
 def solution(mesh):
+    line_of_four = mesh.shape["patch"] == 8 and mesh.shape["expert"] == 4
     in_specs = (
         P("expert", "patch", None),
         P("expert", "patch", None),
@@ -149,5 +535,5 @@
     )
     out_specs = (P("expert", "patch", None), P("expert", "patch", None))
     return jax.shard_map(
-        on_device, mesh=mesh, in_specs=in_specs, out_specs=out_specs, check_vma=False
-    )
+        on_line if line_of_four else on_device, mesh=mesh, in_specs=in_specs, out_specs=out_specs, check_vma=False
+    )

time: 192 us -> 118 us (0.61)
  waiting for transfers between devices: 115 us -> 0 us
  Pallas kernels: 0 us -> 102 us
  matrix products: 24.6 us -> 0 us
  other arithmetic: 13.7 us -> 0 us
  between operations: 14 us -> 0.64 us
  starting transfers between devices: 7.27 us -> 0 us
  local copies, waits for them, and re-layouts: 16.3 us -> 14.2 us
    pallas_call x0 -> x1, Pallas kernels: none -> 102 us  [on_line(): pl.pallas_call(functools.partial(block_kernel, capacity), out_shape=(jax....]
    all_gather x3 -> x0, waiting for transfers between devices: 94.3 us -> none  [the longest x1 51 us: on_device(): lax.all_gather(w_out, 'patch', axis=1, tiled=True)]
    dot_general x10 -> x0, matrix products: 24.6 us -> none  [the longest x1 6 us: expert_block(): jnp.dot(flat_rows, weight_in, preferred_element_type=jnp.float32)]
    all_to_all x2 -> x0, waiting for transfers between devices: 18.5 us -> none  [the longest x1 9.74 us: expert_block(): lax.all_to_all(produced.reshape(expert_count, capacity, width), 'expert',...]
    unnamed x32 -> x6, local copies, waits for them, and re-layouts: 2.43 us -> 14.2 us
    reduce_sum x9 -> x0, other arithmetic: 8.71 us -> none  [the longest x1 3.34 us: attend_keys(): mass = mass * decay + jnp.sum(fresh, axis=-1)]
    slice x6 -> x0, local copies, waits for them, and re-layouts: 8.21 us -> none  [the longest x2 5.88 us: scores_of(): kv_rows[:, :attn_width].reshape(kv_rows.shape[0], head_count, head_size)]
    all_to_all x2 -> x0, starting transfers between devices: 7.16 us -> none  [the longest x1 3.67 us: expert_block(): lax.all_to_all(produced.reshape(expert_count, capacity, width), 'expert',...]
  transfers between devices with their start and end apart: 5 -> 0, of which waited for: 5 -> 0; matrix products, arithmetic and copies ran while one was open for 22% -> 0% of each run, Pallas kernels for 0% -> 0%
where the time goes in v1:
time: 118 us; the launch traced here: 116 us
  Pallas kernels  102 us (86%)
  local copies, waits for them, and re-layouts  14.2 us (12%)
    pallas_call x1, Pallas kernels, on_line(): pl.pallas_call(functools.partial(block_kernel, capacity), out_shape=(jax....  102 us
    unnamed x6, local copies, waits for them, and re-layouts  14.2 us

profile of v1, /device:TPU:1, one launch (start us, length us, event | category | flops | bytes accessed | tf_op | source)
XLA Modules:
  0.0 116.4 jit_solution(675886362728502601)
XLA Ops:
  0.6 1.4 %copy.16 = f32[1,6,1152]{2,1,0:T(8,128)} copy(f32[1,6,1152]{2,0,1:T(1,128)} %param.11) | data formatting | bytes 55296
  2.0 1.4 %copy.11 = s32[1,1,128,2]{3,2,1,0:T(8,128)} copy(s32[1,1,128,2]{2,3,1,0:T(2,128)} %param.12) | data formatting | bytes 2048 | tf_op args[3]
  3.4 1.6 %copy.13.router_ref = bf16[1152,4]{1,0:T(8,128)(2,1)} copy(bf16[1152,4]{0,1:T(4,128)(2,1)} %param.15) | data formatting | bytes 18432 | tf_op args[6]
  5.0 6.4 %copy.12.wqkv_hbm = bf16[1152,1728]{1,0:T(8,128)(2,1)} copy(bf16[1152,1728]{0,1:T(8,128)(2,1)} %param.13) | data formatting | bytes 7962624 | tf_op args[4]
  11.4 101.5 %shard_map.104 = (bf16[128,1152]{1,0:T(8,128)(2,1)}, bf16[128,1152]{1,0:T(8,128)(2,1)}) custom-call(bf16[128,1152]{1,0:T(8,128)(2,1)} %bitcast.12, bf16[128,1152]{1,0:T(8,128)(2,1)} %bitcast.13, f32[6,1152]{1,0:T(8,128)} %bitcast.17, s32[128,2]{1,0:T(8,128)} %bitcast.16, bf16[1152,1728]{1,0:T(8,128)(2,1)} %copy.12.wqkv_hbm, bf16[576,1152]{1,0:T(8,128)(2,1)} %wattn_hbm.1, ...), custom_call_target="tpu_custom_call" | custom-call | tf_op jit(solution)/shard_map/pallas_call | solution.py:484
  113.0 1.7 %copy.19 = bf16[1,128,1152]{2,1,0:T(8,128)(2,1)} copy(bf16[1,128,1152]{2,1,0:T(8,128)(2,1)} %bitcast.15) | data formatting | bytes 589824
  114.7 1.7 %copy.20 = bf16[1,128,1152]{2,1,0:T(8,128)(2,1)} copy(bf16[1,128,1152]{2,1,0:T(8,128)(2,1)} %bitcast.14) | data formatting | bytes 589824

commit v2 on v1

--- a/solution.py
+++ b/solution.py
@@ -141,13 +141,14 @@
 
 MESH = pl.DeviceIdType.MESH
 TO_PARTNER, TO_MIDDLE, TO_CORE = 0, 1, 2
+CHUNKS = 3
 
 
 def block_kernel(
     capacity,
     latent_ref, stale_ref, mod_ref, routes_ref, wqkv_hbm, wattn_hbm, router_ref, win_hbm, wout_hbm,
     out_ref, fresh_ref,
-    kv, wqkv, wattn, win, wout, outgoing, rows, hidden, partial, produced, returned, attended,
+    kv, wqkv, wattn, win, wout, outgoing, rows, hidden, produced, returned, attended,
     load_sem, send_sem, recv_sem, go_send, go_recv, back_send, back_recv,
 ):
     patch, expert = lax.axis_index("patch"), lax.axis_index("expert")
@@ -161,11 +162,15 @@
     tokens, width = latent_ref.shape
     attn = wattn_hbm.shape[0]
     head_size = attn // HEADS
-    experts = router_ref.shape[1]
+    experts = router_ref.shape[0]
     ffw = win_hbm.shape[1]
 
-    buffers = (kv, win, wout)
-    owned = (stale_ref, win_hbm, wout_hbm)
+    chunk = width // CHUNKS
+    chunks = range(2, 2 + CHUNKS)
+    buffers = [kv, win] + [wout.at[part] for part in range(CHUNKS)]
+    owned = [stale_ref, win_hbm] + [
+        wout_hbm.at[:, pl.ds(part * chunk, chunk)] for part in range(CHUNKS)
+    ]
 
     def slot(which, index):
         count = owned[which].shape[0]
@@ -191,13 +196,15 @@
     )
     load_qkv.start()
     load_attn.start()
-    own_in = pltpu.make_async_copy(win_hbm, slot(1, patch), load_sem.at[2])
-    own_out = pltpu.make_async_copy(wout_hbm, slot(2, patch), load_sem.at[3])
+    own_loads = [
+        pltpu.make_async_copy(owned[which], slot(which, patch), load_sem.at[1 + which])
+        for which in range(1, 2 + CHUNKS)
+    ]
 
     @pl.when(middle_plane)
     def _():
-        own_in.start()
-        own_out.start()
+        for load in own_loads:
+            load.start()
 
     barrier = pltpu.get_barrier_semaphore()
     peers = [(other, expert), (partner, expert), (across, expert)]
@@ -214,20 +221,25 @@
     @pl.when(middle_plane)
     def _():
         transfer(0, TO_MIDDLE, patch, True).start()
+        transfer(1, TO_MIDDLE, patch, True).start()
 
     @pl.when(end_plane)
     def _():
-        transfer(1, TO_PARTNER, patch, True).start()
-        transfer(2, TO_PARTNER, patch, True).start()
+        for which in range(1, 2 + CHUNKS):
+            transfer(which, TO_PARTNER, patch, True).start()
 
     def row_of(index):
-        return mod_ref[index : index + 1, :]
+        return mod_ref[index]
+
+    def times_rows(left, right):
+        return lax.dot_general(
+            left, right, (((1,), (1,)), ((), ())), preferred_element_type=jnp.float32
+        )
 
     normed = normalize(latent_ref[...], row_of(0), row_of(1))
     load_qkv.wait()
-    merged = jnp.dot(normed, wqkv[...], preferred_element_type=jnp.float32)
-    query = merged[:, : wattn.shape[0]].astype(jnp.bfloat16)
-    current = merged[:, attn:].astype(jnp.bfloat16)
+    query = times_rows(normed, wqkv[: wattn.shape[0], :]).astype(jnp.bfloat16)
+    current = times_rows(normed, wqkv[attn:, :]).astype(jnp.bfloat16)
     fresh_ref[...] = current
     kv[pl.ds(pl.multiple_of(patch * tokens, 16), tokens), :] = current
 
@@ -239,13 +251,10 @@
         arrived(0, across)
         transfer(0, TO_PARTNER, across).start()
         transfer(0, TO_CORE, across).start()
-        transfer(1, TO_MIDDLE, patch, True).start()
-        transfer(1, TO_CORE, patch, True).start()
         arrived(0, far)
         transfer(0, TO_PARTNER, far).start()
         transfer(0, TO_CORE, far).start()
         transfer(2, TO_MIDDLE, patch, True).start()
-        transfer(2, TO_CORE, patch, True).start()
 
     @pl.when(end_plane)
     def _():
@@ -265,9 +274,7 @@
         chosen = jnp.where(
             (column >= low) & (column < high), query[:, start:stop].astype(jnp.float32), 0.0
         ).astype(jnp.bfloat16)
-        scores = lax.dot_general(
-            chosen, kv[:, start:stop], (((1,), (1,)), ((), ())), preferred_element_type=jnp.float32
-        ) * head_size ** (-0.5)
+        scores = times_rows(chosen, kv[:, start:stop]) * head_size ** (-0.5)
         weights = jnp.exp(scores - jnp.max(scores, axis=-1, keepdims=True))
         total = jnp.sum(weights, axis=-1, keepdims=True)
         low, high = attn + low, attn + high
@@ -284,12 +291,20 @@
         old = attended[:, first : first + stop - start]
         keep = (column < low) & (column >= attn)
         attended[:, first : first + stop - start] = jnp.where(keep, old, mine)
+        if head == HEADS // 2 - 1:
+
+            @pl.when(middle_plane)
+            def _():
+                arrived(1, partner)
+                transfer(1, TO_MIDDLE, partner).start()
+                transfer(1, TO_CORE, partner).start()
+                transfer(1, TO_CORE, patch, True).start()
 
     @pl.when(middle_plane)
     def _():
-        arrived(1, partner)
-        transfer(1, TO_MIDDLE, partner).start()
-        transfer(1, TO_CORE, partner).start()
+        arrived(2, partner)
+        transfer(2, TO_MIDDLE, partner).start()
+        transfer(3, TO_MIDDLE, patch, True).start()
 
     load_attn.wait()
     wattn[:lead, :] = jnp.zeros((lead, width), jnp.bfloat16)
@@ -299,19 +314,18 @@
     middle = (latent_ref[...].astype(jnp.float32) + row_of(2) * projected).astype(jnp.bfloat16)
     out_ref[...] = middle
     normed_two = normalize(middle, row_of(3), row_of(4))
-    logits = jnp.dot(normed_two, router_ref[...], preferred_element_type=jnp.float32)
-
-    lane = lax.broadcasted_iota(jnp.int32, (tokens, 128), 1)
+    logits = times_rows(normed_two, router_ref[...])
+
     line = lax.broadcasted_iota(jnp.int32, (tokens, tokens), 0)
-    before = lax.broadcasted_iota(jnp.int32, (tokens, tokens), 1) < line
-    named = ((routes_ref[:, 0:1] == lane) | (routes_ref[:, 1:2] == lane)).astype(jnp.float32)
-    place = jnp.dot(
-        before.astype(jnp.float32).astype(jnp.bfloat16),
+    lane = lax.broadcasted_iota(jnp.int32, (tokens, tokens), 1)
+    named = ((routes_ref[0:1, :] == line) | (routes_ref[1:2, :] == line)).astype(jnp.float32)
+    place_t = jnp.dot(
         named.astype(jnp.bfloat16),
+        (line < lane).astype(jnp.float32).astype(jnp.bfloat16),
         preferred_element_type=jnp.float32,
     )
-    place = jnp.where(named > 0.0, place, -1.0)
-    place_t = place.T
+    place_t = jnp.where(named > 0.0, place_t, -1.0)
+    place = place_t.T
     entry = lax.broadcasted_iota(jnp.int32, (capacity, tokens), 0).astype(jnp.float32)
     for index in range(experts):
         pick = (entry == place_t[index : index + 1, :]).astype(jnp.float32).astype(jnp.bfloat16)
@@ -332,12 +346,12 @@
             device_id_type=MESH,
         )
 
-    def back(side, index):
+    def back(side, index, part):
         return pltpu.make_async_remote_copy(
-            src_ref=produced.at[span(side * experts + index)],
-            dst_ref=returned.at[span(expert)],
-            send_sem=back_send.at[side, index],
-            recv_sem=back_recv.at[expert],
+            src_ref=produced.at[part, span(side * experts + index)],
+            dst_ref=returned.at[part, span(expert)],
+            send_sem=back_send.at[part, side, index],
+            recv_sem=back_recv.at[part, expert],
             device_id=(partner if side else patch, index),
             device_id_type=MESH,
         )
@@ -349,9 +363,11 @@
             go_recv.at[side, source],
         ).wait()
 
-    def await_back(source):
+    def await_back(source, part):
         pltpu.make_async_copy(
-            outgoing.at[span(source)], returned.at[span(source)], back_recv.at[source]
+            produced.at[part, span(source)],
+            returned.at[part, span(source)],
+            back_recv.at[part, source],
         ).wait()
 
     @pl.when(end_plane)
@@ -364,15 +380,19 @@
         for step in range(1, experts):
             go(0, (expert + step) % experts).start()
         rows[span(expert), :] = outgoing[span(expert), :]
-        arrived(2, partner)
-        transfer(2, TO_MIDDLE, partner).start()
-        transfer(2, TO_CORE, partner).start()
-        for which in (1,):
-            for index in (across, far):
-                arrived(which, index)
-                transfer(which, TO_CORE, index).start()
-        own_in.wait()
-        own_out.wait()
+        for which in chunks[1:]:
+            arrived(which, partner)
+            transfer(which, TO_MIDDLE, partner).start()
+            if which + 1 in chunks:
+                transfer(which + 1, TO_MIDDLE, patch, True).start()
+        for index in (across, far):
+            arrived(1, index)
+            transfer(1, TO_CORE, index).start()
+        for which in chunks:
+            transfer(which, TO_CORE, patch, True).start()
+            transfer(which, TO_CORE, partner).start()
+        for load in own_loads:
+            load.wait()
         for step in range(1, experts):
             await_rows(0, (expert + step) % experts)
         for step in range(experts):
@@ -390,55 +410,49 @@
 
         lax.fori_loop(0, ffw // 256, first_layer, 0)
 
-        half = ffw // 2
-        near_at = pl.multiple_of((z // 2) * half, 128)
-        far_at = pl.multiple_of((1 - z // 2) * half, 128)
-        arrived(2, other)
-        arrived(2, partner + 1 - 2 * core)
-        partial[...] = jnp.dot(
-            hidden[:, pl.ds(near_at, half)],
-            wout[pl.ds(near_at, half), :],
-            preferred_element_type=jnp.float32,
-        )
-        for index in (across, far):
-            arrived(2, index)
-            transfer(2, TO_CORE, index).start()
-        arrived(2, across + 1 - 2 * core)
-        arrived(2, far + 1 - 2 * core)
         count = experts * capacity
-        for side in (1, 0):
-            block = slice(side * count, (side + 1) * count)
-            produced[block, :] = (
-                partial[block, :]
-                + jnp.dot(
-                    hidden[block, pl.ds(far_at, half)],
-                    wout[pl.ds(far_at, half), :],
-                    preferred_element_type=jnp.float32,
-                )
-            ).astype(jnp.bfloat16)
-            for step in range(1 - side, experts):
-                back(side, (expert + step) % experts).start()
-        returned[span(expert), :] = produced[span(expert), :]
-        for step in range(1, experts):
-            await_back((expert + step) % experts)
-
-    @pl.when(end_plane)
-    def _():
-        for step in range(experts):
-            await_back((expert + step) % experts)
-
-    mixture = jnp.zeros((tokens, width), jnp.float32)
+        for part in range(CHUNKS):
+            which = part + 2
+            for index in (across, far):
+                arrived(which, index)
+                transfer(which, TO_CORE, index).start()
+            for plane in range(4):
+                arrived(which, plane * 2 + 1 - core)
+            for side in (1, 0):
+                block = slice(side * count, (side + 1) * count)
+                produced[part, block, :] = jnp.dot(
+                    hidden[block, :], wout[part], preferred_element_type=jnp.float32
+                ).astype(jnp.bfloat16)
+                for step in range(1 - side, experts):
+                    back(side, (expert + step) % experts, part).start()
+            returned[part, span(expert), :] = produced[part, span(expert), :]
+
     entry = lax.broadcasted_iota(jnp.int32, (tokens, capacity), 1).astype(jnp.float32)
     gates = jax.nn.sigmoid(logits)
-    for index in range(experts):
-        pick = (entry == place[:, index : index + 1]).astype(jnp.float32).astype(jnp.bfloat16)
-        picked = jnp.dot(
-            pick,
-            returned[index * capacity : (index + 1) * capacity, :],
-            preferred_element_type=jnp.float32,
-        )
-        mixture = mixture + picked * gates[:, index : index + 1]
-    out_ref[...] = (out_ref[...].astype(jnp.float32) + row_of(5) * mixture).astype(jnp.bfloat16)
+    picks = [
+        (entry == place[:, index : index + 1]).astype(jnp.float32).astype(jnp.bfloat16)
+        for index in range(experts)
+    ]
+    for part in range(CHUNKS):
+        for step in range(1, experts):
+            await_back((expert + step) % experts, part)
+
+        @pl.when(end_plane)
+        def _():
+            await_back(expert, part)
+
+        columns = slice(part * chunk, (part + 1) * chunk)
+        mixture = jnp.zeros((tokens, chunk), jnp.float32)
+        for index in range(experts):
+            picked = jnp.dot(
+                picks[index],
+                returned[part, index * capacity : (index + 1) * capacity, :],
+                preferred_element_type=jnp.float32,
+            )
+            mixture = mixture + picked * gates[:, index : index + 1]
+        out_ref[:, columns] = (
+            out_ref[:, columns].astype(jnp.float32) + row_of(5)[:, columns] * mixture
+        ).astype(jnp.bfloat16)
 
     transfer(0, TO_PARTNER, patch, True).wait_send()
     transfer(0, TO_CORE, patch, True).wait_send()
@@ -447,8 +461,8 @@
 
     @pl.when(end_plane)
     def _():
-        transfer(1, TO_PARTNER, patch, True).wait_send()
-        transfer(2, TO_PARTNER, patch, True).wait_send()
+        for which in range(1, 2 + CHUNKS):
+            transfer(which, TO_PARTNER, patch, True).wait_send()
         for step in range(experts):
             go(1, (expert + step) % experts).wait_send()
 
@@ -458,7 +472,7 @@
         transfer(0, TO_MIDDLE, partner).wait_send()
         transfer(0, TO_PARTNER, across).wait_send()
         transfer(0, TO_PARTNER, far).wait_send()
-        for which in (1, 2):
+        for which in range(1, 2 + CHUNKS):
             transfer(which, TO_MIDDLE, patch, True).wait_send()
             transfer(which, TO_MIDDLE, partner).wait_send()
             transfer(which, TO_CORE, patch, True).wait_send()
@@ -466,9 +480,10 @@
                 transfer(which, TO_CORE, index).wait_send()
         for step in range(1, experts):
             go(0, (expert + step) % experts).wait_send()
-            back(0, (expert + step) % experts).wait_send()
-        for step in range(experts):
-            back(1, (expert + step) % experts).wait_send()
+        for part in range(CHUNKS):
+            for side in (1, 0):
+                for step in range(1 - side, experts):
+                    back(side, (expert + step) % experts, part).wait_send()
 
 
 def on_line(latent, stale_kv, modulation, routes, w_qkv, w_attn_out, router, w_in, w_out):
@@ -491,31 +506,30 @@
         out_specs=(vmem, vmem),
         scratch_shapes=[
             pltpu.VMEM((patches * tokens, 2 * attn), narrow),
-            pltpu.VMEM(w_qkv.shape, narrow),
+            pltpu.VMEM(w_qkv.shape[::-1], narrow),
             pltpu.VMEM((padded, width), narrow),
             pltpu.VMEM((width, ffw), narrow),
-            pltpu.VMEM((ffw, width), narrow),
+            pltpu.VMEM((CHUNKS, ffw, width // CHUNKS), narrow),
             pltpu.VMEM((slots, width), narrow),
             pltpu.VMEM((2 * slots, width), narrow),
             pltpu.VMEM((2 * slots, ffw), narrow),
-            pltpu.VMEM((2 * slots, width), jnp.float32),
-            pltpu.VMEM((2 * slots, width), narrow),
-            pltpu.VMEM((slots, width), narrow),
+            pltpu.VMEM((CHUNKS, 2 * slots, width // CHUNKS), narrow),
+            pltpu.VMEM((CHUNKS, slots, width // CHUNKS), narrow),
             pltpu.VMEM((tokens, padded), jnp.float32),
-            pltpu.SemaphoreType.DMA((4,)),
-            pltpu.SemaphoreType.DMA((3, 3, patches)),
-            pltpu.SemaphoreType.DMA((3, patches)),
+            pltpu.SemaphoreType.DMA((3 + CHUNKS,)),
+            pltpu.SemaphoreType.DMA((2 + CHUNKS, 3, patches)),
+            pltpu.SemaphoreType.DMA((2 + CHUNKS, patches)),
             pltpu.SemaphoreType.DMA((experts,)),
             pltpu.SemaphoreType.DMA((2, experts)),
-            pltpu.SemaphoreType.DMA((2, experts)),
-            pltpu.SemaphoreType.DMA((experts,)),
+            pltpu.SemaphoreType.DMA((CHUNKS, 2, experts)),
+            pltpu.SemaphoreType.DMA((CHUNKS, experts)),
         ],
         compiler_params=pltpu.CompilerParams(
             collective_id=0, has_side_effects=True, vmem_limit_bytes=56 * 1024 * 1024
         ),
     )(
-        latent[0], stale_kv[0], modulation[0], routes[0, 0], w_qkv, w_attn_out, router,
-        w_in[0], w_out[0],
+        latent[0], stale_kv[0], jnp.transpose(modulation, (1, 0, 2)), routes[0, 0].T, w_qkv.T,
+        w_attn_out, router.T, w_in[0], w_out[0],
     )
     return (state[None], current[None])
 

time: 118 us -> 99.4 us (0.84)
  local copies, waits for them, and re-layouts: 14.2 us -> 3.4 us
  Pallas kernels: 102 us -> 94 us
    unnamed x6 -> x2, local copies, waits for them, and re-layouts: 14.2 us -> 3.4 us
    pallas_call x1, Pallas kernels: 102 us -> 94 us  [on_line(): pl.pallas_call(functools.partial(block_kernel, capacity), out_shape=(jax....]
where the time goes in v2:
time: 99.4 us; the launch traced here: 98 us
  Pallas kernels  94 us (95%)
  local copies, waits for them, and re-layouts  3.4 us (3%)
    pallas_call x1, Pallas kernels, on_line(): pl.pallas_call(functools.partial(block_kernel, capacity), out_shape=(jax....  94 us
    unnamed x2, local copies, waits for them, and re-layouts  3.4 us

profile of v2, /device:TPU:1, one launch (start us, length us, event | category | flops | bytes accessed | tf_op | source)
XLA Modules:
  0.0 98.0 jit_solution(1020996538146994576)
XLA Ops:
  0.6 94.0 %shard_map.104 = (bf16[128,1152]{1,0:T(8,128)(2,1)}, bf16[128,1152]{1,0:T(8,128)(2,1)}) custom-call(bf16[128,1152]{1,0:T(8,128)(2,1)} %bitcast.15, bf16[128,1152]{1,0:T(8,128)(2,1)} %bitcast.16, f32[6,1,1152]{2,1,0:T(1,128)} %bitcast.19, s32[2,128]{1,0:T(2,128)} %bitcast.21, bf16[1728,1152]{1,0:T(8,128)(2,1)} %bitcast.12, bf16[576,1152]{1,0:T(8,128)(2,1)} %wattn_hbm.1, ...), custom_call_target="tpu_custom_call" | custom-call | tf_op jit(solution)/shard_map/pallas_call | solution.py:499
  94.6 1.7 %copy.13 = bf16[1,128,1152]{2,1,0:T(8,128)(2,1)} copy(bf16[1,128,1152]{2,1,0:T(8,128)(2,1)} %bitcast.18) | data formatting | bytes 589824
  96.3 1.7 %copy.14 = bf16[1,128,1152]{2,1,0:T(8,128)(2,1)} copy(bf16[1,128,1152]{2,1,0:T(8,128)(2,1)} %bitcast.17) | data formatting | bytes 589824

commit v3 on v2

--- a/solution.py
+++ b/solution.py
@@ -221,12 +221,6 @@
     @pl.when(middle_plane)
     def _():
         transfer(0, TO_MIDDLE, patch, True).start()
-        transfer(1, TO_MIDDLE, patch, True).start()
-
-    @pl.when(end_plane)
-    def _():
-        for which in range(1, 2 + CHUNKS):
-            transfer(which, TO_PARTNER, patch, True).start()
 
     def row_of(index):
         return mod_ref[index]
@@ -248,6 +242,7 @@
         arrived(0, partner)
         transfer(0, TO_MIDDLE, partner).start()
         transfer(0, TO_CORE, partner).start()
+        transfer(1, TO_MIDDLE, patch, True).start()
         arrived(0, across)
         transfer(0, TO_PARTNER, across).start()
         transfer(0, TO_CORE, across).start()
@@ -258,7 +253,10 @@
 
     @pl.when(end_plane)
     def _():
-        for index in (partner, far, across):
+        transfer(0, TO_PARTNER, patch, True).wait_send()
+        transfer(1, TO_PARTNER, patch, True).start()
+        transfer(2, TO_PARTNER, patch, True).start()
+        for index in (partner, across, far):
             arrived(0, index)
             transfer(0, TO_CORE, index).start()
 
@@ -300,6 +298,11 @@
                 transfer(1, TO_CORE, partner).start()
                 transfer(1, TO_CORE, patch, True).start()
 
+            @pl.when(end_plane)
+            def _():
+                transfer(3, TO_PARTNER, patch, True).start()
+                transfer(4, TO_PARTNER, patch, True).start()
+
     @pl.when(middle_plane)
     def _():
         arrived(2, partner)
@@ -454,7 +457,6 @@
             out_ref[:, columns].astype(jnp.float32) + row_of(5)[:, columns] * mixture
         ).astype(jnp.bfloat16)
 
-    transfer(0, TO_PARTNER, patch, True).wait_send()
     transfer(0, TO_CORE, patch, True).wait_send()
     for index in (partner, across, far):
         transfer(0, TO_CORE, index).wait_send()
@@ -468,6 +470,7 @@
 
     @pl.when(middle_plane)
     def _():
+        transfer(0, TO_PARTNER, patch, True).wait_send()
         transfer(0, TO_MIDDLE, patch, True).wait_send()
         transfer(0, TO_MIDDLE, partner).wait_send()
         transfer(0, TO_PARTNER, across).wait_send()
@@ -484,6 +487,11 @@
             for side in (1, 0):
                 for step in range(1 - side, experts):
                     back(side, (expert + step) % experts, part).wait_send()
+
+
+def store_kernel(state_ref, current_ref, out_ref, fresh_ref):
+    out_ref[...] = state_ref[...]
+    fresh_ref[...] = current_ref[...]
 
 
 def on_line(latent, stale_kv, modulation, routes, w_qkv, w_attn_out, router, w_in, w_out):
@@ -531,6 +539,15 @@
         latent[0], stale_kv[0], jnp.transpose(modulation, (1, 0, 2)), routes[0, 0].T, w_qkv.T,
         w_attn_out, router.T, w_in[0], w_out[0],
     )
+    state, current = pl.pallas_call(
+        store_kernel,
+        out_shape=(
+            jax.ShapeDtypeStruct(state.shape, narrow),
+            jax.ShapeDtypeStruct(current.shape, narrow),
+        ),
+        in_specs=[vmem, vmem],
+        out_specs=(vmem, vmem),
+    )(state, current)
     return (state[None], current[None])
 
 

time: 99.4 us -> 92.4 us (0.930); the launches traced: 98 us -> 92.3 us
  local copies, waits for them, and re-layouts: 3.4 us -> 0 us
  Pallas kernels: 94 us -> 91.6 us
    pallas_call x1, Pallas kernels: 94 us -> 89.7 us  [on_line(): pl.pallas_call(functools.partial(block_kernel, capacity), out_shape=(jax....]
    unnamed x2 -> x0, local copies, waits for them, and re-layouts: 3.4 us -> none
    pallas_call x0 -> x1, Pallas kernels: none -> 1.88 us  [on_line(): pl.pallas_call(store_kernel, out_shape=(jax.ShapeDtypeStruct(state.shape,...]
where the time goes in v3:
time: 92.4 us; the launch traced here: 92.3 us
  Pallas kernels  91.6 us (99%)
    pallas_call x1, Pallas kernels, on_line(): pl.pallas_call(functools.partial(block_kernel, capacity), out_shape=(jax....  89.7 us
    pallas_call x1, Pallas kernels, on_line(): pl.pallas_call(store_kernel, out_shape=(jax.ShapeDtypeStruct(state.shape,...  1.88 us

profile of v3, /device:TPU:1, one launch (start us, length us, event | category | flops | bytes accessed | tf_op | source)
XLA Modules:
  0.0 92.3 jit_solution(10552099629835551519)
XLA Ops:
  0.6 89.7 %shard_map.104 = (bf16[128,1152]{1,0:T(8,128)(2,1)}, bf16[128,1152]{1,0:T(8,128)(2,1)}) custom-call(bf16[128,1152]{1,0:T(8,128)(2,1)} %bitcast.15, bf16[128,1152]{1,0:T(8,128)(2,1)} %bitcast.16, f32[6,1,1152]{2,1,0:T(1,128)} %bitcast.17, s32[2,128]{1,0:T(2,128)} %bitcast.19, bf16[1728,1152]{1,0:T(8,128)(2,1)} %bitcast.12, bf16[576,1152]{1,0:T(8,128)(2,1)} %wattn_hbm.1, ...), custom_call_target="tpu_custom_call" | custom-call | tf_op jit(solution)/shard_map/pallas_call | solution.py:507
  90.4 1.9 %shard_map.105 = (bf16[128,1152]{1,0:T(8,128)(2,1)}, bf16[128,1152]{1,0:T(8,128)(2,1)}) custom-call(bf16[128,1152]{1,0:T(8,128)(2,1)} %get-tuple-element.6.state_ref, bf16[128,1152]{1,0:T(8,128)(2,1)} %get-tuple-element.7.current_ref), custom_call_target="tpu_custom_call" | custom-call | tf_op jit(solution)/shard_map/pallas_call | solution.py:542

commit v4 on v3

--- a/solution.py
+++ b/solution.py
@@ -421,13 +421,19 @@
                 transfer(which, TO_CORE, index).start()
             for plane in range(4):
                 arrived(which, plane * 2 + 1 - core)
-            for side in (1, 0):
-                block = slice(side * count, (side + 1) * count)
+            half = count // 2
+            for begin, size in ((count, half), (count + half, half), (0, count)):
+                block = slice(begin, begin + size)
                 produced[part, block, :] = jnp.dot(
                     hidden[block, :], wout[part], preferred_element_type=jnp.float32
                 ).astype(jnp.bfloat16)
-                for step in range(1 - side, experts):
-                    back(side, (expert + step) % experts, part).start()
+                if begin:
+                    first = (begin - count) // capacity
+                    for index in range(first, first + experts // 2):
+                        back(1, index, part).start()
+                else:
+                    for step in range(1, experts):
+                        back(0, (expert + step) % experts, part).start()
             returned[part, span(expert), :] = produced[part, span(expert), :]
 
     entry = lax.broadcasted_iota(jnp.int32, (tokens, capacity), 1).astype(jnp.float32)

time: 92.4 us -> 91.3 us (0.988); the launches traced: 92.3 us -> 89.5 us
  Pallas kernels: 91.6 us -> 88.9 us
    pallas_call x1, Pallas kernels: 89.7 us -> 87 us  [on_line(): pl.pallas_call(functools.partial(block_kernel, capacity), out_shape=(jax....]
where the time goes in v4:
time: 91.3 us; the launch traced here: 89.5 us
  Pallas kernels  88.9 us (97%)
    pallas_call x1, Pallas kernels, on_line(): pl.pallas_call(functools.partial(block_kernel, capacity), out_shape=(jax....  87 us
    pallas_call x1, Pallas kernels, on_line(): pl.pallas_call(store_kernel, out_shape=(jax.ShapeDtypeStruct(state.shape,...  1.88 us

profile of v4, /device:TPU:1, one launch (start us, length us, event | category | flops | bytes accessed | tf_op | source)
XLA Modules:
  0.0 89.5 jit_solution(9742801764402195053)
XLA Ops:
  0.6 87.0 %shard_map.104 = (bf16[128,1152]{1,0:T(8,128)(2,1)}, bf16[128,1152]{1,0:T(8,128)(2,1)}) custom-call(bf16[128,1152]{1,0:T(8,128)(2,1)} %bitcast.15, bf16[128,1152]{1,0:T(8,128)(2,1)} %bitcast.16, f32[6,1,1152]{2,1,0:T(1,128)} %bitcast.17, s32[2,128]{1,0:T(2,128)} %bitcast.19, bf16[1728,1152]{1,0:T(8,128)(2,1)} %bitcast.12, bf16[576,1152]{1,0:T(8,128)(2,1)} %wattn_hbm.1, ...), custom_call_target="tpu_custom_call" | custom-call | tf_op jit(solution)/shard_map/pallas_call | solution.py:513
  87.7 1.9 %shard_map.105 = (bf16[128,1152]{1,0:T(8,128)(2,1)}, bf16[128,1152]{1,0:T(8,128)(2,1)}) custom-call(bf16[128,1152]{1,0:T(8,128)(2,1)} %get-tuple-element.6.state_ref, bf16[128,1152]{1,0:T(8,128)(2,1)} %get-tuple-element.7.current_ref), custom_call_target="tpu_custom_call" | custom-call | tf_op jit(solution)/shard_map/pallas_call | solution.py:548
